TPU v7x, 256 devices: a whole 4x4x8 slice. The times are simulated.
256 devices in a mesh: ab: 16 (over z, y_lo), cd: 8 (over y_hi, x), rep: 2 (over core).
Axes of the slice: x: 4, y: 4 (y_hi: 2, y_lo: 2; y = y_hi * 2 + y_lo), z: 8, core: 2. Of those that a mesh axis runs over, the one named last changes fastest.
Arguments:
- integrals: bfloat16 [36864, 2048], P('ab', ('cd', 'rep')), may hold values from -0.125 to 0.125
- amplitudes: bfloat16 [13824, 2048], P(('cd', 'rep'), 'ab'), may hold values from -6 to 6
Outputs:
- ladder: bfloat16 [13824, 36864], P(('cd', 'rep'), 'ab')
All inputs are finite; a program needn't handle non-finite values.
Results may differ from a plain program's by a relative error of at most 0.001.
Values may be sent and summed in bfloat16 or wider, within the bound.
A program may use at most 64 MiB of HBM per device.

v0:
```python
import jax
import jax.numpy as jnp
from jax import lax
from jax.sharding import PartitionSpec as P


def contract(amplitude_cols, incoming):
    return lax.dot_general(
        amplitude_cols, incoming, (((1,), (1,)), ((), ())), preferred_element_type=jnp.float32
    )


def on_device(integrals, amplitudes):
    whole_amps = lax.all_gather(amplitudes, "ab", axis=1, tiled=True)
    summed = contract(whole_amps, lax.all_gather(integrals, ("cd", "rep"), axis=1, tiled=True))
    return summed.astype(jnp.bfloat16)


def solution(mesh):
    in_specs = (P("ab", ("cd", "rep")), P(("cd", "rep"), "ab"))
    out_specs = P(("cd", "rep"), "ab")
    return jax.shard_map(
        on_device, mesh=mesh, in_specs=in_specs, out_specs=out_specs, check_vma=False
    )
```

profile of v0, /device:TPU:1, one launch (start us, length us, event | category | flops | bytes accessed | tf_op | source)
XLA Modules:
  0.0 235.2 jit_solution(13095949546596803047)
XLA Ops:
  6.5 0.0 all-gather.3.cloned.1.call-start
  6.5 0.7 all-gather.3.cloned.1.call-update
  7.3 0.0 all-gather.5.cloned.1.call-start
  7.3 0.7 all-gather.5.cloned.1.call-update
  8.0 105.0 %all-gather.3.cloned.1.call-done = bf16[864,2048]{1,0:T(8,128)(2,1)} async-done(((bf16[864,128]{1,0:T(8,128)(2,1)}), bf16[864,2048]{1,0:T(8,128)(2,1)}) %all-gather.3.cloned.1.call-update) | async-done | bytes 3538960 | tf_op jit(solution)/shard_map/all_gather | solution.py:14
  113.0 101.2 %all-gather.5.cloned.1.call-done = bf16[2304,2048]{1,0:T(8,128)(2,1)} async-done(((bf16[2304,128]{1,0:T(8,128)(2,1)}), bf16[2304,2048]{1,0:T(8,128)(2,1)}) %all-gather.5.cloned.1.call-update) | async-done | bytes 9437200 | tf_op jit(solution)/shard_map/all_gather | solution.py:15
  214.2 14.1 %convolution_convert_fusion = bf16[864,2304]{1,0:T(8,128)(2,1)} fusion(bf16[864,2048]{1,0:T(8,128)(2,1)} %all-gather.3.cloned.1.call-done, bf16[2304,2048]{1,0:T(8,128)(2,1)} %all-gather.5.cloned.1.call-done), kind=kOutput, calls=%fused_computation | convolution fusion | flops 8155717632 | bytes 16957440 | tf_op jit(solution)/shard_map/dot_general | solution.py:8
Async XLA Ops:
  6.5 106.4 %all-gather.3.cloned.1.call-start = ((), (), s32[]{:S(2)}) async-start(), calls=%async_computation | async-start | bytes 3760128 | tf_op jit(solution)/shard_map/all_gather | solution.py:14
  7.3 206.9 %all-gather.5.cloned.1.call-start = ((), (), s32[]{:S(2)}) async-start(), calls=%async_computation.1 | async-start | bytes 10027008 | tf_op jit(solution)/shard_map/all_gather | solution.py:15
Sparse Core Ops, SparseCore 0:
  9.1 103.8 all-gather.2
  115.5 98.5 all-gather.4
where the time goes:
time: 235 us
  waiting for transfers between devices  208 us (89%)
  matrix products  14.1 us (6%)
  between operations  13.4 us (6%)
    all_gather x1, waiting for transfers between devices, on_device(): whole_amps = lax.all_gather(amplitudes, 'ab', axis=1, tiled=True)  105 us
    all_gather x1, waiting for transfers between devices, on_device(): lax.all_gather(integrals, ('cd', 'rep'), axis=1, tiled=True)  101 us
    dot_general x1, matrix products, contract(): lax.dot_general(amplitude_cols, incoming, (((1,), (1,)), ((), ())), prefe...  14.1 us
  transfers between devices with their start and end apart: 2, of which 2 were waited for; matrix products, arithmetic and copies ran while one was open for 0% of the time, Pallas kernels for 0%

commit v1 on v0

v1 whole, which is shorter than its diff:
```python
import jax
import jax.numpy as jnp
from jax import lax
from jax.experimental import pallas as pl
from jax.experimental.pallas import tpu as pltpu
from jax.sharding import PartitionSpec as P

MESH = pl.DeviceIdType.MESH
ROWS = 864
COLS = 2304
BLK = 128
TILE = 256
NT = COLS // TILE
NA = 4
NB = NT - NA
ACH = 288
QP, QM, QY, QZ = 22, 23, 18, 21
AHEAD = 3
YLAG = 4
SLOTS = 24


def kernel(v_ref, r_ref, o_ref, vbuf, abuf, acc, lsem, xs, xr, ys, yr, ps, pr, zs, zr, cs, cr, os, orr):
    ab, cd, c = lax.axis_index("ab"), lax.axis_index("cd"), lax.axis_index("rep")
    z, yl = ab // 2, lax.rem(ab, 2)
    h, x = cd // 4, lax.rem(cd, 4)

    right, left = (ab, h * 4 + lax.rem(x + 1, 4), c), (ab, h * 4 + lax.rem(x + 3, 4), c)
    across = (ab, (1 - h) * 4 + x, c)
    pair = (z * 2 + 1 - yl, cd, c)
    up, down = (lax.rem(z + 1, 8) * 2 + yl, cd, c), (lax.rem(z + 7, 8) * 2 + yl, cd, c)
    sibling = (ab, cd, 1 - c)

    def remote(src, dst, s, r, to):
        return pltpu.make_async_remote_copy(
            src_ref=src, dst_ref=dst, send_sem=s, recv_sem=r, device_id=to, device_id_type=MESH
        )

    def where(conds, last):
        out = last
        for cond, value in reversed(conds):
            out = jnp.where(cond, value, out)
        return out

    def block(dx, dh):
        hh = h + dh - 2 * h * dh
        return hh * 4 + lax.rem(x + dx, 4)

    def tile_at(j, core, tile):
        return vbuf.at[2 * j + core, pl.ds(pl.multiple_of(tile * TILE, TILE), TILE)]

    def xp(q):
        dx = where([(q < 9, 0), (q < 13, 3), (q < 18, 0)], 3)
        dh = jnp.where(q < 13, 0, 1)
        return dx, dh, q - where([(q < 9, 0), (q < 18, 9)], 18)

    def xm(q):
        dx = where([(q < 9, 0), (q < 14, 1), (q < 18, 0)], 1)
        dh = jnp.where(q < 14, 0, 1)
        return dx, dh, where([(q < 5, q + 4), (q < 14, q - 5)], q - 14)

    def yx(p):
        first = p < 9
        i = jnp.where(first, p, p - 9)
        odd = lax.rem(i, 2)
        dx = jnp.where(first, 0, jnp.where(odd == 1, 3, 1))
        return dx, 0, jnp.where(odd == 1, i // 2, NA + i // 2)

    def xp_copy(q, shift=0, core=c):
        dx, dh, tile = xp(q)
        t = tile_at(block(dx + shift, dh), core, tile)
        return remote(t, t, xs.at[0, q], xr.at[0, q], right)

    def xm_copy(q, shift=0, core=c):
        dx, dh, tile = xm(q)
        t = tile_at(block(dx + shift, dh), core, tile)
        return remote(t, t, xs.at[1, q], xr.at[1, q], left)

    def y_copy(p, flip=0, core=c):
        dx, _, tile = yx(p)
        t = tile_at(block(dx, flip), core, tile)
        return remote(t, t, ys.at[p], yr.at[p], across)

    def a_at(zz, y, chunk):
        return abuf.at[2 * zz + y, pl.ds(pl.multiple_of(chunk * ACH, 16), ACH)]

    def zpart(r, way):
        k = r - 18
        lastp = jnp.where(k == 2, 1, 0) if way == 0 else jnp.where(k >= 1, 1, 0)
        lastc = jnp.where(k == 2, 0, k) if way == 0 else jnp.where(k == 0, 2, k)
        late = r >= 18
        part = jnp.where(late, lastp, lax.rem(r, 6) // 3)
        return r // 6 + 1, part, jnp.where(late, lastc, lax.rem(r, 3))

    def z_copy(s, way):
        k = s - 18
        if way == 0:
            tail = 12 + k + jnp.where(k == 2, 1, 0)
        else:
            tail = 14 + k + jnp.where(k >= 1, 1, 0)
        rr = jnp.where(s < 18, s, tail + 6)
        back, part, chunk = rr // 6, lax.rem(rr, 6) // 3, lax.rem(rr, 3)
        zz = lax.rem(z + (8 - back if way == 0 else back), 8)
        t = a_at(zz, jnp.where(part == 1, 1 - yl, yl), chunk)
        return remote(t, t, zs.at[way, s], zr.at[way, s], up if way == 0 else down)

    def z_arrival(r, way):
        back, part, chunk = zpart(r, way)
        zz = lax.rem(z + (8 - back if way == 0 else back), 8)
        t = a_at(zz, jnp.where(part == 1, 1 - yl, yl), chunk)
        return remote(t, t, zs.at[way, r], zr.at[way, r], up if way == 0 else down)

    def sib_copy(stream, q, core):
        if stream == 0:
            dx, dh, tile = xp(q)
            dx = dx + 3
        elif stream == 1:
            dx, dh, tile = xm(q)
            dx = dx + 1
        else:
            dx, _, tile = yx(q)
            dh = 1
        t = tile_at(block(dx, dh), core, tile)
        return remote(t, t, cs.at[stream, q], cr.at[stream, q], sibling)

    def pair_copy(i, y):
        t = a_at(z, y, i)
        return remote(t, t, ps.at[i], pr.at[i], pair)

    own_v = pltpu.make_async_copy(v_ref, vbuf.at[2 * cd + c], lsem.at[0])
    own_a = pltpu.make_async_copy(r_ref, abuf.at[2 * z + yl], lsem.at[1])
    own_a.start()
    own_v.start()

    barrier = pltpu.get_barrier_semaphore()
    for other in (right, left, across, pair, up, down, sibling):
        pl.semaphore_signal(barrier, inc=1, device_id=other, device_id_type=MESH)
    pl.semaphore_wait(barrier, 7)

    own_a.wait()
    for i in range(3):
        pair_copy(i, yl).start()
        z_copy(jnp.int32(i), 0).start()
        z_copy(jnp.int32(i), 1).start()
    own_v.wait()
    for i in range(AHEAD):
        xp_copy(jnp.int32(i)).start()
        xm_copy(jnp.int32(i)).start()
        if i < 2:
            y_copy(jnp.int32(i)).start()
    mine = vbuf.at[2 * cd + c]
    theirs = vbuf.at[2 * cd + 1 - c]
    remote(mine, mine, os.at[0], orr.at[0], sibling).start()
    acc[...] = jnp.zeros_like(acc)

    def product(j, tile, n):
        a = jnp.concatenate([abuf[2 * j], abuf[2 * j + 1]], axis=1)
        rows = pl.ds(pl.multiple_of(tile * TILE, TILE), n * TILE)
        b = jnp.concatenate([vbuf[2 * j, rows], vbuf[2 * j + 1, rows]], axis=1)
        return lax.dot_general(a, b, (((1,), (1,)), ((), ())), preferred_element_type=jnp.float32)

    def add(j, tile, n):
        part = product(j, tile, n)
        for k in range(n):
            acc[tile + k] += part[:, k * TILE : (k + 1) * TILE]

    def clip(v, top):
        return jnp.minimum(jnp.maximum(v, 0), top)

    def a_slot(j):
        d = lax.rem(j - z + 8, 8)
        d = jnp.minimum(d, 8 - d)
        return where([(d == 0, 3), (d == 1, 6), (d == 2, 13), (d == 3, 20)], SLOTS)

    def counts(j, t):
        jh, jx = j // 4, lax.rem(j, 4)
        dx = lax.rem(jx - x + 4, 4)
        nq, np_ = clip(t - 1, QM), clip(t - 5, QY)
        y1 = jnp.minimum(np_, 9)
        y2 = clip(np_ - 9, 9)
        same = jh == h
        first = where(
            [(same, where([(dx == 0, NA), (dx == 3, clip(nq, NA)), (dx == 1, clip(nq - 5, NA))], clip(nq - 9, NA))),
             (dx == 0, y1 // 2), (dx == 3, y2 // 2), (dx == 1, clip(nq - 14, NA))],
            clip(nq - 18, NA))
        second = where(
            [(same, where([(dx == 0, NB), (dx == 3, clip(nq - 4, NB)), (dx == 1, clip(nq, NB))], clip(nq - 9, NB))),
             (dx == 0, (y1 + 1) // 2), (dx == 3, clip(nq - 13, NB)), (dx == 1, (y2 + 1) // 2)],
            clip(nq - 18, NB))
        return first, second

    def zcount(t):
        return jnp.minimum(((t + 1) * 25) // 28, QZ)

    def xp_sent(t):
        return jnp.minimum(jnp.minimum(t + 1 + AHEAD, QP), 18 + jnp.maximum((t - 12) // 2, 0))

    def xm_sent(t):
        return jnp.minimum(jnp.minimum(t + 1 + AHEAD, QM), 18 + jnp.maximum((t - 11) // 2, 0))

    def slot(t, _):
        @pl.when(t < QP)
        def _():
            xp_copy(t, 3).wait_recv()
            sib_copy(0, t, c).start()

        @pl.when(t < QM)
        def _():
            xm_copy(t, 1).wait_recv()
            sib_copy(1, t, c).start()

        p = t - YLAG

        @pl.when(jnp.logical_and(p >= 0, p < QY))
        def _():
            y_copy(p, 1).wait_recv()
            sib_copy(2, p, c).start()

        def send(copy, lo, hi):
            def one(q, _):
                copy(q).start()
                return 0

            lax.fori_loop(lo, hi, one, 0)

        send(xp_copy, xp_sent(t - 1), xp_sent(t))
        send(xm_copy, xm_sent(t - 1), xm_sent(t))
        send(y_copy, jnp.minimum(t + 2, QY), jnp.minimum(t + 3, QY))

        def zstep(r, _):
            z_arrival(r, 0).wait_recv()
            z_arrival(r, 1).wait_recv()

            @pl.when(r < 3)
            def _():
                pair_copy(r, 1 - yl).wait_recv()

            @pl.when(r + 3 < QZ)
            def _():
                z_copy(r + 3, 0).start()
                z_copy(r + 3, 1).start()

            return 0

        lax.fori_loop(zcount(t - 1), zcount(t), zstep, 0)

        @pl.when(t == 0)
        def _():
            remote(theirs, theirs, os.at[0], orr.at[0], sibling).wait_recv()

        for stream, q, top in ((0, t - 1, QP), (1, t - 1, QM), (2, p - 1, QY)):

            @pl.when(jnp.logical_and(q >= 0, q < top))
            def _(stream=stream, q=q):
                sib_copy(stream, q, 1 - c).wait_recv()

        n_new = where([(t == 3, 1), (t == 6, 2), (t == 13, 2), (t == 20, 2)], 0)
        dist = where([(t == 3, 0), (t == 6, 1), (t == 13, 2)], 3)

        def catch_up(i, _):
            j = lax.rem(z + jnp.where(i == 0, dist, 8 - dist), 8)
            first, second = counts(j, t)

            def run(lo, n):
                def three(k, _):
                    add(j, lo + 3 * k, 3)
                    return 0

                lax.fori_loop(0, n // 3, three, 0)

                def one(k, _):
                    add(j, k, 1)
                    return 0

                lax.fori_loop(lo + 3 * (n // 3), lo + n, one, 0)

            whole = first == NA

            def part(k, _):
                lo = jnp.where(k == 0, 0, NA)
                run(lo, jnp.where(k == 0, jnp.where(whole, NA + second, first), second))
                return 0

            lax.fori_loop(0, jnp.where(whole, 1, 2), part, 0)
            return 0

        lax.fori_loop(0, n_new, catch_up, 0)

        def fresh(i, _):
            q = jnp.where(i == 2, p - 1, t - 1)
            dxp, dhp, tp = xp(q)
            dxm, dhm, tm = xm(q)
            dxy, _, ty = yx(q)
            dx = where([(i == 0, dxp + 3), (i == 1, dxm + 1)], dxy)
            dh = where([(i == 0, dhp), (i == 1, dhm)], 1)
            tile = where([(i == 0, tp), (i == 1, tm)], ty)
            top = where([(i == 0, QP), (i == 1, QM)], QY)
            j = block(dx, dh)

            @pl.when((q >= 0) & (q < top) & (a_slot(j) <= t))
            def _():
                add(j, tile, 1)

            return 0

        lax.fori_loop(0, 3, fresh, 0)
        return 0

    lax.fori_loop(0, SLOTS, slot, 0)

    j = lax.rem(z + 4, 8)

    def last(i, _):
        part = product(j, 3 * i, 3)
        for k in range(3):
            cols = pl.ds(pl.multiple_of((3 * i + k) * TILE, TILE), TILE)
            o_ref[:, cols] = (acc[3 * i + k] + part[:, k * TILE : (k + 1) * TILE]).astype(o_ref.dtype)
        return 0

    lax.fori_loop(0, NT // 3, last, 0)

    remote(mine, mine, os.at[0], orr.at[0], sibling).wait_send()

    def drain(top, *copies):
        def one(q, _):
            for copy in copies:
                copy(q).wait_send()
            return 0

        lax.fori_loop(0, top, one, 0)

    drain(QP, xp_copy, lambda q: sib_copy(0, q, c))
    drain(QM, xm_copy, lambda q: sib_copy(1, q, c))
    drain(QY, y_copy, lambda q: sib_copy(2, q, c))
    drain(QZ, lambda s: z_copy(s, 0), lambda s: z_copy(s, 1))
    drain(3, lambda i: pair_copy(i, yl))


def on_device(integrals, amplitudes):
    dma = pltpu.SemaphoreType.DMA
    return pl.pallas_call(
        kernel,
        out_shape=jax.ShapeDtypeStruct((ROWS, COLS), jnp.bfloat16),
        in_specs=[pl.BlockSpec(memory_space=pl.ANY)] * 2,
        out_specs=pl.BlockSpec(memory_space=pltpu.VMEM),
        scratch_shapes=[
            pltpu.VMEM((16, COLS, BLK), jnp.bfloat16),
            pltpu.VMEM((16, ROWS, BLK), jnp.bfloat16),
            pltpu.VMEM((NT, ROWS, TILE), jnp.float32),
            dma((2,)),
            dma((2, QM)), dma((2, QM)),
            dma((QY,)), dma((QY,)),
            dma((3,)), dma((3,)),
            dma((2, QZ)), dma((2, QZ)),
            dma((3, QM)), dma((3, QM)),
            dma((1,)), dma((1,)),
        ],
        compiler_params=pltpu.CompilerParams(
            collective_id=0, has_side_effects=True, vmem_limit_bytes=56 << 20
        ),
        cost_estimate=pl.CostEstimate(
            flops=2 * ROWS * COLS * 2048, bytes_accessed=5 << 20, transcendentals=0
        ),
        name="ladder",
    )(integrals, amplitudes)


def solution(mesh):
    in_specs = (P("ab", ("cd", "rep")), P(("cd", "rep"), "ab"))
    out_specs = P(("cd", "rep"), "ab")
    return jax.shard_map(on_device, mesh=mesh, in_specs=in_specs, out_specs=out_specs, check_vma=False)
```

time: 235 us -> 66.3 us (0.28)
  waiting for transfers between devices: 208 us -> 0 us
  Pallas kernels: 0 us -> 61.9 us
  matrix products: 14.1 us -> 0 us
  between operations: 13.4 us -> 0.01 us
  local copies, waits for them, and re-layouts: 0 us -> 4.32 us
    all_gather x2 -> x0, waiting for transfers between devices: 206 us -> none  [the longest x1 105 us: on_device(): whole_amps = lax.all_gather(amplitudes, 'ab', axis=1, tiled=True)]
    pallas_call x0 -> x1, Pallas kernels: none -> 61.9 us  [on_device(): pl.pallas_call(kernel, out_shape=jax.ShapeDtypeStruct((ROWS, COLS), jnp.b...]
    dot_general x1 -> x0, matrix products: 14.1 us -> none  [contract(): lax.dot_general(amplitude_cols, incoming, (((1,), (1,)), ((), ())), prefe...]
    unnamed x0 -> x1, local copies, waits for them, and re-layouts: none -> 4.32 us
  transfers between devices with their start and end apart: 2 -> 0, of which waited for: 2 -> 0; matrix products, arithmetic and copies ran while one was open for 0% -> 0% of each run, Pallas kernels for 0% -> 0%
where the time goes in v1:
time: 66.3 us; the launch traced here: 66.2 us
  Pallas kernels  61.9 us (93%)
  local copies, waits for them, and re-layouts  4.32 us (7%)
    pallas_call x1, Pallas kernels, on_device(): pl.pallas_call(kernel, out_shape=jax.ShapeDtypeStruct((ROWS, COLS), jnp.b...  61.9 us
    unnamed x1, local copies, waits for them, and re-layouts  4.32 us

profile of v1, /device:TPU:1, one launch (start us, length us, event | category | flops | bytes accessed | tf_op | source)
XLA Modules:
  0.0 66.2 jit_solution(14935502630893970134)
XLA Ops:
  0.0 61.9 %ladder.1 = bf16[864,2304]{1,0:T(8,128)(2,1)} custom-call(bf16[2304,128]{1,0:T(8,128)(2,1)} %v_ref.1, bf16[864,128]{1,0:T(8,128)(2,1)} %r_ref.1), custom_call_target="tpu_custom_call" | custom-call | flops 8153726976 | bytes 5242880 | tf_op jit(solution)/shard_map/ladder/pallas_call | solution.py:341
  61.9 4.3 %copy.4 = bf16[864,2304]{1,0:T(8,128)(2,1)} copy(bf16[864,2304]{1,0:T(8,128)(2,1)} %ladder.1) | data formatting | bytes 7962624

commit v2 on v0

v2 whole, which is shorter than its diff:
```python
import jax
import jax.numpy as jnp
from jax import lax
from jax.experimental import pallas as pl
from jax.experimental.pallas import tpu as pltpu
from jax.sharding import PartitionSpec as P

MESH = pl.DeviceIdType.MESH
ROWS = 864
COLS = 2304
BLK = 128
TILE = 256
NT = COLS // TILE
ACH = 288
QX, QY, QZ = 23, 17, 21
AHEAD = 6
YAHEAD = 4
ZAHEAD = 3
XSEM, ZSEM, CSEM = 2 * AHEAD, 2 * ZAHEAD, 4
YLAG = 4
SLOTS = QX + 1


def z_count(t):
    return ((t + 1) * 25) // 28


OWN_SLOT, *A_SLOTS = [next(t for t in range(99) if z_count(t) >= n) for n in (3, 6, 12, 18)]
OWN_TILES = (3, 4, 5, 2, 1, 0, 6, 7, 8)
XP_HERE = [0] * 9 + [0, 1, 2, 3, 4] + [YLAG + p for p in (1, 2, 6, 7, 8, 9, 10, 13, 14)]
XM_HERE = [0] * 9 + [0, 1, 2, 3] + [YLAG + p for p in (1, 0, 3, 4, 5)] + [13] + [YLAG + p for p in (11, 12, 15, 16)]
XP_GROUPS = {2: 3, 5: 3, 8: 3, 11: 3, 13: 2, 16: 3, 18: 2, 21: 3, 22: 1}
XM_GROUPS = {1: 2, 4: 3, 7: 3, 8: 1, 10: 2, 12: 2, 14: 2, 17: 3, 18: 1, 20: 2, 22: 2}
Y_GROUPS = {2: 3, 5: 3, 8: 3, 10: 2, 12: 2, 14: 2, 16: 2}


def kernel(v_ref, r_ref, o_ref, vbuf, abuf, acc, lsem, xs, xr, ys, yr, ps, pr, zs, zr, cs, cr, orr):
    ab, cd, c = lax.axis_index("ab"), lax.axis_index("cd"), lax.axis_index("rep")
    z, yl = ab // 2, lax.rem(ab, 2)
    h, x = cd // 4, lax.rem(cd, 4)

    right, left = (ab, h * 4 + lax.rem(x + 1, 4), c), (ab, h * 4 + lax.rem(x + 3, 4), c)
    across = (ab, (1 - h) * 4 + x, c)
    pair = (z * 2 + 1 - yl, cd, c)
    up, down = (lax.rem(z + 1, 8) * 2 + yl, cd, c), (lax.rem(z + 7, 8) * 2 + yl, cd, c)
    sibling = (ab, cd, 1 - c)

    def remote(src, dst, s, r, to):
        return pltpu.make_async_remote_copy(
            src_ref=src, dst_ref=dst, send_sem=s, recv_sem=r, device_id=to, device_id_type=MESH
        )

    def where(conds, last):
        out = last
        for cond, value in reversed(conds):
            out = jnp.where(cond, value, out)
        return out

    def block(dx, dh):
        hh = h + dh - 2 * h * dh
        return hh * 4 + lax.rem(x + dx, 4)

    def tile_at(j, core, tile):
        return vbuf.at[2 * j + core, pl.ds(pl.multiple_of(tile * TILE, TILE), TILE)]

    def xp(q):
        dx = where([(q < 9, 0), (q < 14, 3), (q < 19, 0)], 3)
        dh = jnp.where(q < 14, 0, 1)
        return dx, dh, q - where([(q < 9, 0), (q < 14, 9), (q < 19, 10)], 19)

    def xm(q):
        dx = where([(q < 9, 0), (q < 13, 1), (q < 18, 0)], 1)
        dh = jnp.where(q < 13, 0, 1)
        return dx, dh, where([(q < 9, 8 - q), (q < 18, 17 - q), (q == 18, 4)], 27 - q)

    def yx(p):
        k = jnp.maximum(p - 9, 0)
        up_half = lax.rem(k // 2, 2) == 0
        i = (k // 4) * 2 + lax.rem(k, 2)
        dx = where([(p < 9, 0), (up_half, 3)], 1)
        return dx, 0, where([(p < 3, p + 3), (p < 6, 5 - p), (p < 9, p), (up_half, i)], 8 - i)

    def xp_copy(q, shift=0):
        dx, dh, tile = xp(q)
        t = tile_at(block(dx + shift, dh), c, tile)
        return remote(t, t, xs.at[0], xr.at[0, lax.rem(q, XSEM)], right)

    def xm_copy(q, shift=0):
        dx, dh, tile = xm(q)
        t = tile_at(block(dx + shift, dh), c, tile)
        return remote(t, t, xs.at[1], xr.at[1, lax.rem(q, XSEM)], left)

    def y_copy(p, flip=0):
        dx, _, tile = yx(p)
        t = tile_at(block(dx, flip), c, tile)
        return remote(t, t, ys.at[0], yr.at[p], across)

    def a_at(zz, y, chunk):
        return abuf.at[2 * zz + y, pl.ds(pl.multiple_of(chunk * ACH, 16), ACH)]

    def z_copy(s, way):
        k = s - 18
        if way == 0:
            tail = where([(k == 0, 12), (k == 1, 15)], 13)
        else:
            tail = where([(k == 0, 14), (k == 1, 17)], 16)
        rr = jnp.where(s < 18, s, tail + 6)
        back, part, chunk = rr // 6, lax.rem(rr, 6) // 3, lax.rem(rr, 3)
        zz = lax.rem(z + (8 - back if way == 0 else back), 8)
        t = a_at(zz, jnp.where(part == 1, 1 - yl, yl), chunk)
        return remote(t, t, zs.at[way], zr.at[way, lax.rem(s, ZSEM)], up if way == 0 else down)

    def z_arrival(r, way):
        k = r - 18
        if way == 0:
            part, chunk = jnp.where(k == 1, 1, 0), jnp.where(k == 2, 1, 0)
        else:
            part, chunk = jnp.where(k >= 1, 1, 0), jnp.where(k == 2, 1, 2)
        part = jnp.where(k >= 0, part, lax.rem(r, 6) // 3)
        chunk = jnp.where(k >= 0, chunk, lax.rem(r, 3))
        back = r // 6 + 1
        zz = lax.rem(z + (8 - back if way == 0 else back), 8)
        t = a_at(zz, jnp.where(part == 1, 1 - yl, yl), chunk)
        return remote(t, t, zs.at[way], zr.at[way, lax.rem(r, ZSEM)], up if way == 0 else down)

    def place(stream, q):
        if stream == 0:
            dx, dh, tile = xp(q)
            return block(dx + 3, dh), tile
        if stream == 1:
            dx, dh, tile = xm(q)
            return block(dx + 1, dh), tile
        dx, _, tile = yx(q)
        return block(dx, 1), tile

    def sib_copy(stream, q, core):
        j, tile = place(stream, q)
        t = tile_at(j, core, tile)
        return remote(t, t, cs.at[0], cr.at[stream, lax.rem(q, CSEM)], sibling)

    def pair_copy(i, y):
        t = a_at(z, y, i)
        return remote(t, t, ps.at[0], pr.at[i], pair)

    own_v = pltpu.make_async_copy(v_ref, vbuf.at[2 * cd + c], lsem.at[0])
    own_a = pltpu.make_async_copy(r_ref, abuf.at[2 * z + yl], lsem.at[1])
    own_a.start()
    own_v.start()

    barrier = pltpu.get_barrier_semaphore()
    for other in (right, left, across, pair, up, down, sibling):
        pl.semaphore_signal(barrier, inc=1, device_id=other, device_id_type=MESH)
    pl.semaphore_wait(barrier, 7)

    for i in range(3):
        rows = r_ref.at[pl.ds(i * ACH, ACH)]
        t = a_at(z, yl, i)
        remote(rows, t, ps.at[0], pr.at[i], pair).start()
        remote(rows, t, zs.at[0], zr.at[0, i], up).start()
        remote(rows, t, zs.at[1], zr.at[1, i], down).start()
    mine = vbuf.at[2 * cd + c]
    theirs = vbuf.at[2 * cd + 1 - c]
    for i in range(AHEAD):
        for tile, sem, to in ((i, 0, right), (8 - i, 1, left)):
            rows = v_ref.at[pl.ds(tile * TILE, TILE)]
            remote(rows, tile_at(cd, c, tile), xs.at[sem], xr.at[sem, i], to).start()
        if i < YAHEAD:
            tile = OWN_TILES[i]
            rows = v_ref.at[pl.ds(tile * TILE, TILE)]
            remote(rows, tile_at(cd, c, tile), ys.at[0], yr.at[i], across).start()
    remote(v_ref, mine, cs.at[0], orr.at[0], sibling).start()
    acc[...] = jnp.zeros_like(acc)
    own_a.wait()
    own_v.wait()

    def product(a, j, tile, n):
        rows = pl.ds(pl.multiple_of(tile * TILE, TILE), n * TILE)
        b = jnp.concatenate([vbuf[2 * j, rows], vbuf[2 * j + 1, rows]], axis=1)
        return lax.dot_general(a, b, (((1,), (1,)), ((), ())), preferred_element_type=jnp.float32)

    def add(j, tile, n):
        part = product(jnp.concatenate([abuf[2 * j], abuf[2 * j + 1]], axis=1), j, tile, n)
        for k in range(n):
            acc[tile + k] += part[:, k * TILE : (k + 1) * TILE]

    def clip(v, top):
        return jnp.minimum(jnp.maximum(v, 0), top)

    def a_slot(j):
        d = lax.rem(j - z + 8, 8)
        d = jnp.minimum(d, 8 - d)
        return where([(d == 0, OWN_SLOT), (d == 1, A_SLOTS[0]), (d == 2, A_SLOTS[1]), (d == 3, A_SLOTS[2])], SLOTS)

    def counts(j, t, run):
        jh, jx = j // 4, lax.rem(j, 4)
        dx = lax.rem(jx - x + 4, 4)
        nq, np_ = clip(t - 1, QX), clip(t - 1 - YLAG, QY)
        y1, y2 = jnp.minimum(np_, 9), clip(np_ - 9, 8)
        ya, yb = clip(y2, 2) + clip(y2 - 4, 2), clip(y2 - 2, 2) + clip(y2 - 6, 2)
        same = jh == h
        at0, at1, at3 = dx == 0, dx == 1, dx == 3

        def pick(near, far):
            return jnp.where(same, where([(at0, near[0]), (at1, near[1]), (at3, near[3])], near[2]),
                             where([(at0, far[0]), (at1, far[1]), (at3, far[3])], far[2]))

        n9 = clip(nq, 9)
        lo1 = pick((0, 9 - n9, 0, 0), (3 - clip(y1 - 3, 3), 5 - clip(nq - 13, 5), 0, 0))
        hi1 = pick((NT, NT, clip(nq - 9, 5), n9), (3 + clip(y1, 3), 5, clip(nq - 19, 4), ya))
        lo2 = pick((NT, NT, NT, NT), (6, NT, 4, 4))
        hi2 = pick((NT, NT, NT, NT), (6 + clip(y1 - 6, 3), NT, 4 + clip(nq - 18, 1), 4 + clip(nq - 14, 5)))
        n3 = pick((0, 0, clip(nq - 9, 4), 0), (0, yb, clip(nq - 19, 4), 0))
        lo = where([(run == 0, lo1), (run == 1, lo2)], NT - n3)
        return lo, where([(run == 0, hi1 - lo1), (run == 1, hi2 - lo2)], n3)

    def x_sent(t, here):
        out = jnp.minimum(t + 1 + AHEAD, QX)
        for q, slot in enumerate(here):
            if slot > q - AHEAD:
                out = jnp.minimum(out, jnp.where(t >= slot, QX, q)) if q >= AHEAD else out
        return out

    def y_sent(t):
        return jnp.minimum(t + 1 + YAHEAD, QY)

    def group(q, groups):
        return where([(q == last, n) for last, n in groups.items()], 0)

    def zstep(r, _):
        z_arrival(r, 0).wait_recv()
        z_arrival(r, 1).wait_recv()

        @pl.when(r < 3)
        def _():
            pair_copy(r, 1 - yl).wait_recv()

        @pl.when(r + ZAHEAD < QZ)
        def _():
            z_copy(r + ZAHEAD, 0).start()

        @pl.when((r + ZAHEAD < QZ) & (r != 16))
        def _():
            @pl.when(r == 17)
            def _():
                z_copy(r + ZAHEAD - 1, 1).start()

            z_copy(r + ZAHEAD, 1).start()

        return 0

    def send(copy, lo, hi):
        def one(q, _):
            copy(q).start()
            return 0

        lax.fori_loop(lo, hi, one, 0)

    def slot(t, _):
        p = t - YLAG

        @pl.when(t < QX)
        def _():
            xp_copy(t, 3).wait_recv()
            sib_copy(0, t, c).start()
            xm_copy(t, 1).wait_recv()
            sib_copy(1, t, c).start()

        @pl.when((p >= 0) & (p < QY))
        def _():
            y_copy(p, 1).wait_recv()
            sib_copy(2, p, c).start()

        send(xp_copy, x_sent(t - 1, XP_HERE), x_sent(t, XP_HERE))
        send(xm_copy, x_sent(t - 1, XM_HERE), x_sent(t, XM_HERE))
        send(y_copy, y_sent(t - 1), y_sent(t))
        lax.fori_loop(clip(z_count(t - 1), QZ - 1), clip(z_count(t), QZ - 1), zstep, 0)

        @pl.when(t == 0)
        def _():
            remote(theirs, theirs, cs.at[0], orr.at[0], sibling).wait_recv()

        @pl.when((t >= 1) & (t <= QX))
        def _():
            sib_copy(0, t - 1, 1 - c).wait_recv()
            sib_copy(1, t - 1, 1 - c).wait_recv()

        @pl.when((p >= 1) & (p <= QY))
        def _():
            sib_copy(2, p - 1, 1 - c).wait_recv()

        n_new = where([(t == OWN_SLOT, 1), (t == A_SLOTS[0], 2), (t == A_SLOTS[1], 2), (t == A_SLOTS[2], 2)], 0)
        dist = where([(t == OWN_SLOT, 0), (t == A_SLOTS[0], 1), (t == A_SLOTS[1], 2)], 3)

        def fresh(i):
            q = jnp.where(i == 2, p - 1, t - 1)
            j0, t0 = place(0, q)
            j1, t1 = place(1, q)
            j2, t2 = place(2, q)
            j = where([(i == 0, j0), (i == 1, j1)], j2)
            n = where([(i == 0, group(q, XP_GROUPS)), (i == 1, group(q, XM_GROUPS))], group(q, Y_GROUPS))
            n = jnp.minimum(clip(t - a_slot(j) + 1, 3), n)
            rising = (q < 3) | ((q >= 6) & (q < 11)) | (q == 13) | (q == 14)
            lo = where([(i == 0, t0 - n + 1), (i == 1, t1)], jnp.where(rising, t2 - n + 1, t2))
            return j, lo, n

        def caught_up(i):
            j = lax.rem(z + jnp.where(i < 6, dist, 8 - dist), 8)
            lo, n = counts(j, t, lax.rem(i, 3))
            return j, lo, n

        def work(i, _):
            j, lo, n = lax.cond(i < 3, fresh, caught_up, i)

            def three(k, _):
                add(j, lo + 3 * k, 3)
                return 0

            lax.fori_loop(0, n // 3, three, 0)
            more = lax.rem(n, 3)

            @pl.when(more == 2)
            def _():
                add(j, lo + n - 2, 2)

            @pl.when(more == 1)
            def _():
                add(j, lo + n - 1, 1)

            return 0

        lax.fori_loop(0, 3 + 3 * n_new, work, 0)
        return 0

    lax.fori_loop(0, SLOTS, slot, 0)

    j = lax.rem(z + 4, 8)

    def last(i, _):
        @pl.when(i == 2)
        def _():
            z_arrival(jnp.int32(QZ - 1), 0).wait_recv()
            z_arrival(jnp.int32(QZ - 1), 1).wait_recv()

        chunk = where([(i == 0, 0), (i == 1, 2)], 1)
        rows = pl.ds(pl.multiple_of(chunk * ACH, 16), ACH)
        a = jnp.concatenate([abuf[2 * j, rows], abuf[2 * j + 1, rows]], axis=1)
        for g in range(NT // 3):
            part = product(a, j, 3 * g, 3)
            for k in range(3):
                tile = 3 * g + k
                o_ref[rows, tile * TILE : (tile + 1) * TILE] = (
                    acc[tile, rows] + part[:, k * TILE : (k + 1) * TILE]
                ).astype(o_ref.dtype)
        return 0

    lax.fori_loop(0, 3, last, 0)

    def left_all(ref, sem, to):
        remote(ref, ref, sem, orr.at[0], to).wait_send()

    x_bytes = vbuf.at[pl.ds(0, 4), pl.ds(0, QX * TILE // 4)]
    left_all(x_bytes, xs.at[0], right)
    left_all(x_bytes, xs.at[1], left)
    left_all(vbuf.at[pl.ds(0, 2), pl.ds(0, QY * TILE // 2)], ys.at[0], across)
    left_all(abuf.at[pl.ds(0, QZ * ACH // ROWS)], zs.at[0], up)
    left_all(abuf.at[pl.ds(0, QZ * ACH // ROWS)], zs.at[1], down)
    left_all(abuf.at[0], ps.at[0], pair)
    left_all(vbuf.at[pl.ds(0, ((2 * QX + QY) * TILE + COLS) // COLS)], cs.at[0], sibling)


def on_device(integrals, amplitudes):
    dma = pltpu.SemaphoreType.DMA
    return pl.pallas_call(
        kernel,
        out_shape=pltpu.VMEM((ROWS, COLS), jnp.bfloat16),
        in_specs=[pl.BlockSpec(memory_space=pltpu.HBM)] * 2,
        out_specs=pl.BlockSpec(memory_space=pltpu.VMEM),
        scratch_shapes=[
            pltpu.VMEM((16, COLS, BLK), jnp.bfloat16),
            pltpu.VMEM((16, ROWS, BLK), jnp.bfloat16),
            pltpu.VMEM((NT, ROWS, TILE), jnp.float32),
            dma((2,)),
            dma((2,)), dma((2, XSEM)),
            dma((1,)), dma((QY,)),
            dma((1,)), dma((3,)),
            dma((2,)), dma((2, ZSEM)),
            dma((1,)), dma((3, CSEM)),
            dma((1,)),
        ],
        compiler_params=pltpu.CompilerParams(
            collective_id=0, has_side_effects=True, vmem_limit_bytes=59 << 20
        ),
        cost_estimate=pl.CostEstimate(
            flops=2 * ROWS * COLS * 2048, bytes_accessed=5 << 20, transcendentals=0
        ),
        name="ladder",
    )(integrals, amplitudes)


def solution(mesh):
    in_specs = (P("ab", ("cd", "rep")), P(("cd", "rep"), "ab"))
    out_specs = P(("cd", "rep"), "ab")
    return jax.shard_map(on_device, mesh=mesh, in_specs=in_specs, out_specs=out_specs, check_vma=False)
```

time: 235 us -> 55.9 us (0.24)
  waiting for transfers between devices: 208 us -> 0 us
  Pallas kernels: 0 us -> 53.9 us
  matrix products: 14.1 us -> 0 us
  between operations: 13.4 us -> 0.01 us
    all_gather x2 -> x0, waiting for transfers between devices: 206 us -> none  [the longest x1 105 us: on_device(): whole_amps = lax.all_gather(amplitudes, 'ab', axis=1, tiled=True)]
    pallas_call x0 -> x1, Pallas kernels: none -> 53.9 us  [on_device(): pl.pallas_call(kernel, out_shape=pltpu.VMEM((ROWS, COLS), jnp.bfloat16),...]
    dot_general x1 -> x0, matrix products: 14.1 us -> none  [contract(): lax.dot_general(amplitude_cols, incoming, (((1,), (1,)), ((), ())), prefe...]
  transfers between devices with their start and end apart: 2 -> 0, of which waited for: 2 -> 0; matrix products, arithmetic and copies ran while one was open for 0% -> 0% of each run, Pallas kernels for 0% -> 0%
where the time goes in v2:
time: 55.9 us; the launch traced here: 55.8 us
  Pallas kernels  53.9 us (96%)
  local copies, waits for them, and re-layouts  1.94 us (3%)
    pallas_call x1, Pallas kernels, on_device(): pl.pallas_call(kernel, out_shape=pltpu.VMEM((ROWS, COLS), jnp.bfloat16),...  53.9 us
    unnamed x1, local copies, waits for them, and re-layouts  1.94 us

profile of v2, /device:TPU:1, one launch (start us, length us, event | category | flops | bytes accessed | tf_op | source)
XLA Modules:
  0.0 55.8 jit_solution(1760402518515458356)
XLA Ops:
  0.0 53.9 %ladder.1 = bf16[864,2304]{1,0:T(8,128)(2,1)S(1)} custom-call(bf16[2304,128]{1,0:T(8,128)(2,1)} %v_ref.1, bf16[864,128]{1,0:T(8,128)(2,1)} %r_ref.1), custom_call_target="tpu_custom_call" | custom-call | flops 8153726976 | bytes 5242880 | tf_op jit(solution)/shard_map/ladder/pallas_call | solution.py:373
  53.9 1.9 %copy.4 = bf16[864,2304]{1,0:T(8,128)(2,1)} copy(bf16[864,2304]{1,0:T(8,128)(2,1)S(1)} %ladder.1) | data formatting | bytes 7962624

commit v3 on v2

--- a/solution.py
+++ b/solution.py
@@ -29,8 +29,9 @@
 OWN_TILES = (3, 4, 5, 2, 1, 0, 6, 7, 8)
 XP_HERE = [0] * 9 + [0, 1, 2, 3, 4] + [YLAG + p for p in (1, 2, 6, 7, 8, 9, 10, 13, 14)]
 XM_HERE = [0] * 9 + [0, 1, 2, 3] + [YLAG + p for p in (1, 0, 3, 4, 5)] + [13] + [YLAG + p for p in (11, 12, 15, 16)]
-XP_GROUPS = {2: 3, 5: 3, 8: 3, 11: 3, 13: 2, 16: 3, 18: 2, 21: 3, 22: 1}
-XM_GROUPS = {1: 2, 4: 3, 7: 3, 8: 1, 10: 2, 12: 2, 14: 2, 17: 3, 18: 1, 20: 2, 22: 2}
+
+XP_GROUPS = {2: 3, 5: 3, 8: 3, 13: 5, 18: 5, 21: 3, 22: 1}
+XM_GROUPS = {3: 4, 8: 5, 12: 4, 17: 5, 18: 1, 22: 4}
 Y_GROUPS = {2: 3, 5: 3, 8: 3, 10: 2, 12: 2, 14: 2, 16: 2}
 
 
@@ -191,27 +192,25 @@
         d = jnp.minimum(d, 8 - d)
         return where([(d == 0, OWN_SLOT), (d == 1, A_SLOTS[0]), (d == 2, A_SLOTS[1]), (d == 3, A_SLOTS[2])], SLOTS)
 
-    def counts(j, t, run):
+    def came(j, tile):
         jh, jx = j // 4, lax.rem(j, 4)
         dx = lax.rem(jx - x + 4, 4)
-        nq, np_ = clip(t - 1, QX), clip(t - 1 - YLAG, QY)
-        y1, y2 = jnp.minimum(np_, 9), clip(np_ - 9, 8)
-        ya, yb = clip(y2, 2) + clip(y2 - 4, 2), clip(y2 - 2, 2) + clip(y2 - 6, 2)
-        same = jh == h
-        at0, at1, at3 = dx == 0, dx == 1, dx == 3
-
-        def pick(near, far):
-            return jnp.where(same, where([(at0, near[0]), (at1, near[1]), (at3, near[3])], near[2]),
-                             where([(at0, far[0]), (at1, far[1]), (at3, far[3])], far[2]))
-
-        n9 = clip(nq, 9)
-        lo1 = pick((0, 9 - n9, 0, 0), (3 - clip(y1 - 3, 3), 5 - clip(nq - 13, 5), 0, 0))
-        hi1 = pick((NT, NT, clip(nq - 9, 5), n9), (3 + clip(y1, 3), 5, clip(nq - 19, 4), ya))
-        lo2 = pick((NT, NT, NT, NT), (6, NT, 4, 4))
-        hi2 = pick((NT, NT, NT, NT), (6 + clip(y1 - 6, 3), NT, 4 + clip(nq - 18, 1), 4 + clip(nq - 14, 5)))
-        n3 = pick((0, 0, clip(nq - 9, 4), 0), (0, yb, clip(nq - 19, 4), 0))
-        lo = where([(run == 0, lo1), (run == 1, lo2)], NT - n3)
-        return lo, where([(run == 0, hi1 - lo1), (run == 1, hi2 - lo2)], n3)
+        low = tile < 4
+        pos = where([(tile < 3, 5 - tile), (tile < 6, tile - 3)], tile)
+        rise = where([(tile < 2, 9 + tile)], 11 + tile) + YLAG + 1
+        fall = where([(tile > 6, 19 - tile)], 21 - tile) + YLAG + 1
+        near = where([(dx == 0, 0), (dx == 1, 9 - tile), (dx == 3, tile + 1), (tile < 5, tile + 10)], 18 - tile)
+        far = where(
+            [(dx == 0, pos + YLAG + 1), (dx == 1, jnp.where(tile < 5, 18 - tile, fall)),
+             (dx == 3, jnp.where(low, rise, tile + 11)), (low, tile + 20), (tile == 4, 19)],
+            28 - tile)
+        return jnp.where(jh == h, near, far)
+
+    def all_came(j):
+        dx = lax.rem(lax.rem(j, 4) - x + 4, 4)
+        near = where([(dx == 0, 0), (dx == 2, 14)], 9)
+        far = where([(dx == 0, YLAG + 9), (dx == 3, 19), (dx == 1, YLAG + 17)], QX)
+        return jnp.where(j // 4 == h, near, far)
 
     def x_sent(t, here):
         out = jnp.minimum(t + 1 + AHEAD, QX)
@@ -288,72 +287,67 @@
         def _():
             sib_copy(2, p - 1, 1 - c).wait_recv()
 
-        n_new = where([(t == OWN_SLOT, 1), (t == A_SLOTS[0], 2), (t == A_SLOTS[1], 2), (t == A_SLOTS[2], 2)], 0)
-        dist = where([(t == OWN_SLOT, 0), (t == A_SLOTS[0], 1), (t == A_SLOTS[1], 2)], 3)
-
         def fresh(i):
             q = jnp.where(i == 2, p - 1, t - 1)
-            j0, t0 = place(0, q)
-            j1, t1 = place(1, q)
-            j2, t2 = place(2, q)
-            j = where([(i == 0, j0), (i == 1, j1)], j2)
-            n = where([(i == 0, group(q, XP_GROUPS)), (i == 1, group(q, XM_GROUPS))], group(q, Y_GROUPS))
-            n = jnp.minimum(clip(t - a_slot(j) + 1, 3), n)
-            rising = (q < 3) | ((q >= 6) & (q < 11)) | (q == 13) | (q == 14)
-            lo = where([(i == 0, t0 - n + 1), (i == 1, t1)], jnp.where(rising, t2 - n + 1, t2))
-            return j, lo, n
-
-        def caught_up(i):
-            j = lax.rem(z + jnp.where(i < 6, dist, 8 - dist), 8)
-            lo, n = counts(j, t, lax.rem(i, 3))
-            return j, lo, n
+            full = where([(i == 0, group(q, XP_GROUPS)), (i == 1, group(q, XM_GROUPS))], group(q, Y_GROUPS))
+
+            def due():
+                j0, t0 = place(0, q)
+                j1, t1 = place(1, q)
+                j2, t2 = place(2, q)
+                j = where([(i == 0, j0), (i == 1, j1)], j2)
+                n = jnp.minimum(clip(t - a_slot(j) + 1, 5), full)
+                rising = (q < 3) | ((q >= 6) & (q < 11)) | (q == 13) | (q == 14)
+                lo = where([(i == 0, t0 - n + 1), (i == 1, t1)], jnp.where(rising, t2 - n + 1, t2))
+                return j, lo, n, jnp.int32(0)
+
+            return lax.cond(full > 0, due, lambda: (jnp.int32(0),) * 4)
+
+        event = where([(t < A_SLOTS[0], OWN_SLOT), (t < A_SLOTS[1], A_SLOTS[0]), (t < A_SLOTS[2], A_SLOTS[1])], A_SLOTS[2])
+        dist = where([(t < A_SLOTS[0], 0), (t < A_SLOTS[1], 1), (t < A_SLOTS[2], 2)], 3)
+        busy = (t == event) | ((t == event + 1) & (dist > 0))
+
+        def waited(i):
+            j = lax.rem(z + jnp.where(t == event, dist, 8 - dist), 8)
+            whole = all_came(j) < event
+
+            def part():
+                lo = 3 * (i - 3)
+                b0, b1, b2 = [jnp.where(came(j, lo + m) < event, 1, 0) for m in range(3)]
+                n = b0 + b1 + b2
+                gap = jnp.where((n == 2) & (b1 == 0), 1, 0)
+                return j, lo + jnp.where(b0 == 1, 0, jnp.where(b1 == 1, 1, 2)), n, gap
+
+            return lax.cond(whole, lambda: (j, jnp.int32(0), jnp.where(i == 3, NT, 0), jnp.int32(0)), part)
 
         def work(i, _):
-            j, lo, n = lax.cond(i < 3, fresh, caught_up, i)
-
-            def three(k, _):
-                add(j, lo + 3 * k, 3)
+            j, lo, n, gap = lax.cond(i < 3, fresh, waited, i)
+            for size in (2, 3, 4, 5, NT):
+
+                @pl.when((n == size) & (gap == 0))
+                def _(size=size):
+                    add(j, lo if size < NT else 0, size)
+
+            def one(m, _):
+                add(j, lo + 2 * m, 1)
                 return 0
 
-            lax.fori_loop(0, n // 3, three, 0)
-            more = lax.rem(n, 3)
-
-            @pl.when(more == 2)
-            def _():
-                add(j, lo + n - 2, 2)
-
-            @pl.when(more == 1)
-            def _():
-                add(j, lo + n - 1, 1)
-
+            lax.fori_loop(0, where([(n == 1, 1), (gap == 1, 2)], 0), one, 0)
             return 0
 
-        lax.fori_loop(0, 3 + 3 * n_new, work, 0)
+        lax.fori_loop(0, jnp.where(busy, 6, 3), work, 0)
         return 0
 
     lax.fori_loop(0, SLOTS, slot, 0)
 
     j = lax.rem(z + 4, 8)
 
-    def last(i, _):
-        @pl.when(i == 2)
-        def _():
-            z_arrival(jnp.int32(QZ - 1), 0).wait_recv()
-            z_arrival(jnp.int32(QZ - 1), 1).wait_recv()
-
-        chunk = where([(i == 0, 0), (i == 1, 2)], 1)
-        rows = pl.ds(pl.multiple_of(chunk * ACH, 16), ACH)
-        a = jnp.concatenate([abuf[2 * j, rows], abuf[2 * j + 1, rows]], axis=1)
-        for g in range(NT // 3):
-            part = product(a, j, 3 * g, 3)
-            for k in range(3):
-                tile = 3 * g + k
-                o_ref[rows, tile * TILE : (tile + 1) * TILE] = (
-                    acc[tile, rows] + part[:, k * TILE : (k + 1) * TILE]
-                ).astype(o_ref.dtype)
-        return 0
-
-    lax.fori_loop(0, 3, last, 0)
+    z_arrival(jnp.int32(QZ - 1), 0).wait_recv()
+    z_arrival(jnp.int32(QZ - 1), 1).wait_recv()
+    part = product(jnp.concatenate([abuf[2 * j], abuf[2 * j + 1]], axis=1), j, 0, NT)
+    for k in range(NT):
+        cols = slice(k * TILE, (k + 1) * TILE)
+        o_ref[:, cols] = (acc[k] + part[:, cols]).astype(o_ref.dtype)
 
     def left_all(ref, sem, to):
         remote(ref, ref, sem, orr.at[0], to).wait_send()

time: 55.9 us -> 53.7 us (0.961)
  Pallas kernels: 53.9 us -> 51.7 us
    pallas_call x1, Pallas kernels: 53.9 us -> 51.7 us  [on_device(): pl.pallas_call(kernel, out_shape=pltpu.VMEM((ROWS, COLS), jnp.bfloat16),...]
where the time goes in v3:
time: 53.7 us; the launch traced here: 53.6 us
  Pallas kernels  51.7 us (96%)
  local copies, waits for them, and re-layouts  1.94 us (4%)
    pallas_call x1, Pallas kernels, on_device(): pl.pallas_call(kernel, out_shape=pltpu.VMEM((ROWS, COLS), jnp.bfloat16),...  51.7 us
    unnamed x1, local copies, waits for them, and re-layouts  1.94 us

profile of v3, /device:TPU:1, one launch (start us, length us, event | category | flops | bytes accessed | tf_op | source)
XLA Modules:
  0.0 53.6 jit_solution(85627504285785257)
XLA Ops:
  0.0 51.7 %ladder.1 = bf16[864,2304]{1,0:T(8,128)(2,1)S(1)} custom-call(bf16[2304,128]{1,0:T(8,128)(2,1)} %v_ref.1, bf16[864,128]{1,0:T(8,128)(2,1)} %r_ref.1), custom_call_target="tpu_custom_call" | custom-call | flops 8153726976 | bytes 5242880 | tf_op jit(solution)/shard_map/ladder/pallas_call | solution.py:367
  51.7 1.9 %copy.4 = bf16[864,2304]{1,0:T(8,128)(2,1)} copy(bf16[864,2304]{1,0:T(8,128)(2,1)S(1)} %ladder.1) | data formatting | bytes 7962624

commit v4 on v3

--- a/solution.py
+++ b/solution.py
@@ -19,6 +19,7 @@
 XSEM, ZSEM, CSEM = 2 * AHEAD, 2 * ZAHEAD, 4
 YLAG = 4
 SLOTS = QX + 1
+CUTS = ((0, 3), (3, 6), (6, 9))
 
 
 def z_count(t):
@@ -30,12 +31,12 @@
 XP_HERE = [0] * 9 + [0, 1, 2, 3, 4] + [YLAG + p for p in (1, 2, 6, 7, 8, 9, 10, 13, 14)]
 XM_HERE = [0] * 9 + [0, 1, 2, 3] + [YLAG + p for p in (1, 0, 3, 4, 5)] + [13] + [YLAG + p for p in (11, 12, 15, 16)]
 
-XP_GROUPS = {2: 3, 5: 3, 8: 3, 13: 5, 18: 5, 21: 3, 22: 1}
-XM_GROUPS = {3: 4, 8: 5, 12: 4, 17: 5, 18: 1, 22: 4}
+XP_GROUPS = {2: 3, 5: 3, 8: 3, 13: 5, 18: 5}
+XM_GROUPS = {3: 4, 8: 5, 12: 4, 17: 5}
 Y_GROUPS = {2: 3, 5: 3, 8: 3, 10: 2, 12: 2, 14: 2, 16: 2}
 
 
-def kernel(v_ref, r_ref, o_ref, vbuf, abuf, acc, lsem, xs, xr, ys, yr, ps, pr, zs, zr, cs, cr, orr):
+def kernel(v_ref, r_ref, vbuf, abuf, acc, lsem, xs, xr, ys, yr, ps, pr, zs, zr, cs, cr, orr):
     ab, cd, c = lax.axis_index("ab"), lax.axis_index("cd"), lax.axis_index("rep")
     z, yl = ab // 2, lax.rem(ab, 2)
     h, x = cd // 4, lax.rem(cd, 4)
@@ -202,8 +203,8 @@
         near = where([(dx == 0, 0), (dx == 1, 9 - tile), (dx == 3, tile + 1), (tile < 5, tile + 10)], 18 - tile)
         far = where(
             [(dx == 0, pos + YLAG + 1), (dx == 1, jnp.where(tile < 5, 18 - tile, fall)),
-             (dx == 3, jnp.where(low, rise, tile + 11)), (low, tile + 20), (tile == 4, 19)],
-            28 - tile)
+             (dx == 3, jnp.where(low, rise, tile + 11))],
+            99)
         return jnp.where(jh == h, near, far)
 
     def all_came(j):
@@ -305,10 +306,10 @@
 
         event = where([(t < A_SLOTS[0], OWN_SLOT), (t < A_SLOTS[1], A_SLOTS[0]), (t < A_SLOTS[2], A_SLOTS[1])], A_SLOTS[2])
         dist = where([(t < A_SLOTS[0], 0), (t < A_SLOTS[1], 1), (t < A_SLOTS[2], 2)], 3)
-        busy = (t == event) | ((t == event + 1) & (dist > 0))
+        busy = where([(dist == 0, t == event), (dist == 1, (t == event) | (t == event + 2)), (dist == 2, (t == event + 2) | (t == event + 3))], (t == event) | (t == event + 1))
 
         def waited(i):
-            j = lax.rem(z + jnp.where(t == event, dist, 8 - dist), 8)
+            j = lax.rem(z + jnp.where((t == event) | ((dist == 2) & (t == event + 2)), dist, 8 - dist), 8)
             whole = all_came(j) < event
 
             def part():
@@ -340,14 +341,8 @@
 
     lax.fori_loop(0, SLOTS, slot, 0)
 
-    j = lax.rem(z + 4, 8)
-
     z_arrival(jnp.int32(QZ - 1), 0).wait_recv()
     z_arrival(jnp.int32(QZ - 1), 1).wait_recv()
-    part = product(jnp.concatenate([abuf[2 * j], abuf[2 * j + 1]], axis=1), j, 0, NT)
-    for k in range(NT):
-        cols = slice(k * TILE, (k + 1) * TILE)
-        o_ref[:, cols] = (acc[k] + part[:, cols]).astype(o_ref.dtype)
 
     def left_all(ref, sem, to):
         remote(ref, ref, sem, orr.at[0], to).wait_send()
@@ -362,17 +357,52 @@
     left_all(vbuf.at[pl.ds(0, ((2 * QX + QY) * TILE + COLS) // COLS)], cs.at[0], sibling)
 
 
+def finish(vbuf, abuf, acc, o_ref, out, sem):
+    z, cd = lax.axis_index("ab") // 2, lax.axis_index("cd")
+    far_a = lax.rem(z + 4, 8)
+    far_v = (1 - cd // 4) * 4 + lax.rem(cd + 2, 4)
+    copies = []
+    for g, (lo, hi) in enumerate(CUTS):
+        cols = pl.ds(lo * TILE, (hi - lo) * TILE)
+        copies.append(pltpu.make_async_copy(out.at[:, cols], o_ref.at[:, cols], sem.at[g]))
+
+    def run(blocks):
+        planes = [2 * j + i for j in blocks for i in range(2)]
+        a = jnp.concatenate([abuf[k] for k in planes], axis=1)
+        for (lo, hi), copy in zip(CUTS, copies):
+            rows = pl.ds(lo * TILE, (hi - lo) * TILE)
+            b = jnp.concatenate([vbuf[k, rows] for k in planes], axis=1)
+            part = lax.dot_general(a, b, (((1,), (1,)), ((), ())), preferred_element_type=jnp.float32)
+            for tile in range(lo, hi):
+                cols = slice((tile - lo) * TILE, (tile - lo + 1) * TILE)
+                out[:, tile * TILE : (tile + 1) * TILE] = (acc[tile] + part[:, cols]).astype(out.dtype)
+            copy.start()
+
+    @pl.when(far_a == far_v)
+    def _():
+        run([far_a])
+
+    @pl.when(far_a != far_v)
+    def _():
+        run([far_a, far_v])
+
+    for copy in copies:
+        copy.wait()
+
+
 def on_device(integrals, amplitudes):
     dma = pltpu.SemaphoreType.DMA
-    return pl.pallas_call(
+    args = [pltpu.with_memory_space_constraint(v, pltpu.HBM) for v in (integrals, amplitudes)]
+    held = pl.pallas_call(
         kernel,
-        out_shape=pltpu.VMEM((ROWS, COLS), jnp.bfloat16),
-        in_specs=[pl.BlockSpec(memory_space=pltpu.HBM)] * 2,
-        out_specs=pl.BlockSpec(memory_space=pltpu.VMEM),
-        scratch_shapes=[
+        out_shape=[
             pltpu.VMEM((16, COLS, BLK), jnp.bfloat16),
             pltpu.VMEM((16, ROWS, BLK), jnp.bfloat16),
             pltpu.VMEM((NT, ROWS, TILE), jnp.float32),
+        ],
+        in_specs=[pl.BlockSpec(memory_space=pltpu.HBM)] * 2,
+        out_specs=[pl.BlockSpec(memory_space=pltpu.VMEM)] * 3,
+        scratch_shapes=[
             dma((2,)),
             dma((2,)), dma((2, XSEM)),
             dma((1,)), dma((QY,)),
@@ -382,13 +412,26 @@
             dma((1,)),
         ],
         compiler_params=pltpu.CompilerParams(
-            collective_id=0, has_side_effects=True, vmem_limit_bytes=59 << 20
+            collective_id=0, has_side_effects=True, vmem_limit_bytes=24 << 20
         ),
         cost_estimate=pl.CostEstimate(
-            flops=2 * ROWS * COLS * 2048, bytes_accessed=5 << 20, transcendentals=0
+            flops=2 * ROWS * COLS * 1536, bytes_accessed=1 << 20, transcendentals=0
         ),
         name="ladder",
-    )(integrals, amplitudes)
+    )(*args)
+    held = [pltpu.with_memory_space_constraint(v, pltpu.VMEM) for v in held]
+    return pl.pallas_call(
+        finish,
+        out_shape=jax.ShapeDtypeStruct((ROWS, COLS), jnp.bfloat16),
+        in_specs=[pl.BlockSpec(memory_space=pltpu.VMEM)] * 3,
+        out_specs=pl.BlockSpec(memory_space=pltpu.HBM),
+        scratch_shapes=[pltpu.VMEM((ROWS, COLS), jnp.bfloat16), dma((len(CUTS),))],
+        compiler_params=pltpu.CompilerParams(vmem_limit_bytes=24 << 20),
+        cost_estimate=pl.CostEstimate(
+            flops=2 * ROWS * COLS * 512, bytes_accessed=4 << 20, transcendentals=0
+        ),
+        name="finish",
+    )(*held)
 
 
 def solution(mesh):

time: 53.7 us -> 52.1 us (0.970)
  local copies, waits for them, and re-layouts: 1.94 us -> 0 us
    unnamed x1 -> x0, local copies, waits for them, and re-layouts: 1.94 us -> none
    pallas_call x1 -> x2, Pallas kernels: 51.7 us -> 52 us  [the longest x1 48.6 us: on_device(): pl.pallas_call(kernel, out_shape=[pltpu.VMEM((16, COLS, BLK), jnp.bfloat1...]
where the time goes in v4:
time: 52.1 us; the launch traced here: 52 us
  Pallas kernels  52 us (100%)
    pallas_call x1, Pallas kernels, on_device(): pl.pallas_call(kernel, out_shape=[pltpu.VMEM((16, COLS, BLK), jnp.bfloat1...  48.6 us
    pallas_call x1, Pallas kernels, on_device(): pl.pallas_call(finish, out_shape=jax.ShapeDtypeStruct((ROWS, COLS), jnp.b...  3.43 us

profile of v4, /device:TPU:1, one launch (start us, length us, event | category | flops | bytes accessed | tf_op | source)
XLA Modules:
  0.0 52.0 jit_solution(10323667747476180464)
XLA Ops:
  0.0 48.6 %ladder.1 = (bf16[16,2304,128]{2,1,0:T(8,128)(2,1)S(1)}, bf16[16,864,128]{2,1,0:T(8,128)(2,1)S(1)}, f32[9,864,256]{2,1,0:T(8,128)S(1)}) custom-call(bf16[2304,128]{1,0:T(8,128)(2,1)} %v_ref.1, bf16[864,128]{1,0:T(8,128)(2,1)} %r_ref.1), custom_call_target="tpu_custom_call" | custom-call | flops 6115295232 | bytes 1048576 | tf_op jit(solution)/shard_map/ladder/pallas_call | solution.py:396
  48.6 3.4 %finish.1 = bf16[864,2304]{1,0:T(8,128)(2,1)} custom-call(bf16[16,2304,128]{2,1,0:T(8,128)(2,1)S(1)} %get-tuple-element.8.vbuf, bf16[16,864,128]{2,1,0:T(8,128)(2,1)S(1)} %get-tuple-element.9.abuf, f32[9,864,256]{2,1,0:T(8,128)S(1)} %get-tuple-element.10.acc), custom_call_target="tpu_custom_call" | custom-call | flops 2038431744 | bytes 4194304 | tf_op jit(solution)/shard_map/finish/pallas_call | solution.py:423

commit v5 on v4

--- a/solution.py
+++ b/solution.py
@@ -19,7 +19,7 @@
 XSEM, ZSEM, CSEM = 2 * AHEAD, 2 * ZAHEAD, 4
 YLAG = 4
 SLOTS = QX + 1
-CUTS = ((0, 3), (3, 6), (6, 9))
+CUTS = ((0, 3), (3, 7), (7, 9))
 
 
 def z_count(t):
@@ -28,10 +28,12 @@
 
 OWN_SLOT, *A_SLOTS = [next(t for t in range(99) if z_count(t) >= n) for n in (3, 6, 12, 18)]
 OWN_TILES = (3, 4, 5, 2, 1, 0, 6, 7, 8)
+ZP_HERE = [-1, -1, -1] + list(range(15)) + [12, 13, 15]
+ZM_HERE = [-1, -1, -1] + list(range(15)) + [14, 16, 17]
 XP_HERE = [0] * 9 + [0, 1, 2, 3, 4] + [YLAG + p for p in (1, 2, 6, 7, 8, 9, 10, 13, 14)]
 XM_HERE = [0] * 9 + [0, 1, 2, 3] + [YLAG + p for p in (1, 0, 3, 4, 5)] + [13] + [YLAG + p for p in (11, 12, 15, 16)]
 
-XP_GROUPS = {2: 3, 5: 3, 8: 3, 13: 5, 18: 5}
+XP_GROUPS = {2: 3, 5: 3, 8: 3, 13: 5, 18: 5, 21: 3}
 XM_GROUPS = {3: 4, 8: 5, 12: 4, 17: 5}
 Y_GROUPS = {2: 3, 5: 3, 8: 3, 10: 2, 12: 2, 14: 2, 16: 2}
 
@@ -82,19 +84,19 @@
         dx = where([(p < 9, 0), (up_half, 3)], 1)
         return dx, 0, where([(p < 3, p + 3), (p < 6, 5 - p), (p < 9, p), (up_half, i)], 8 - i)
 
-    def xp_copy(q, shift=0):
+    def xp_copy(q):
         dx, dh, tile = xp(q)
-        t = tile_at(block(dx + shift, dh), c, tile)
+        t = tile_at(block(dx, dh), c, tile)
         return remote(t, t, xs.at[0], xr.at[0, lax.rem(q, XSEM)], right)
 
-    def xm_copy(q, shift=0):
+    def xm_copy(q):
         dx, dh, tile = xm(q)
-        t = tile_at(block(dx + shift, dh), c, tile)
+        t = tile_at(block(dx, dh), c, tile)
         return remote(t, t, xs.at[1], xr.at[1, lax.rem(q, XSEM)], left)
 
-    def y_copy(p, flip=0):
+    def y_copy(p):
         dx, _, tile = yx(p)
-        t = tile_at(block(dx, flip), c, tile)
+        t = tile_at(block(dx, 0), c, tile)
         return remote(t, t, ys.at[0], yr.at[p], across)
 
     def a_at(zz, y, chunk):
@@ -103,27 +105,14 @@
     def z_copy(s, way):
         k = s - 18
         if way == 0:
-            tail = where([(k == 0, 12), (k == 1, 15)], 13)
+            tail = where([(k == 0, 18), (k == 1, 19)], 21)
         else:
-            tail = where([(k == 0, 14), (k == 1, 17)], 16)
-        rr = jnp.where(s < 18, s, tail + 6)
+            tail = where([(k == 0, 20), (k == 1, 22)], 23)
+        rr = jnp.where(s < 18, s, tail)
         back, part, chunk = rr // 6, lax.rem(rr, 6) // 3, lax.rem(rr, 3)
         zz = lax.rem(z + (8 - back if way == 0 else back), 8)
         t = a_at(zz, jnp.where(part == 1, 1 - yl, yl), chunk)
         return remote(t, t, zs.at[way], zr.at[way, lax.rem(s, ZSEM)], up if way == 0 else down)
-
-    def z_arrival(r, way):
-        k = r - 18
-        if way == 0:
-            part, chunk = jnp.where(k == 1, 1, 0), jnp.where(k == 2, 1, 0)
-        else:
-            part, chunk = jnp.where(k >= 1, 1, 0), jnp.where(k == 2, 1, 2)
-        part = jnp.where(k >= 0, part, lax.rem(r, 6) // 3)
-        chunk = jnp.where(k >= 0, chunk, lax.rem(r, 3))
-        back = r // 6 + 1
-        zz = lax.rem(z + (8 - back if way == 0 else back), 8)
-        t = a_at(zz, jnp.where(part == 1, 1 - yl, yl), chunk)
-        return remote(t, t, zs.at[way], zr.at[way, lax.rem(r, ZSEM)], up if way == 0 else down)
 
     def place(stream, q):
         if stream == 0:
@@ -135,10 +124,15 @@
         dx, _, tile = yx(q)
         return block(dx, 1), tile
 
-    def sib_copy(stream, q, core):
+    def sib_copy(stream, q):
         j, tile = place(stream, q)
-        t = tile_at(j, core, tile)
+        t = tile_at(j, c, tile)
         return remote(t, t, cs.at[0], cr.at[stream, lax.rem(q, CSEM)], sibling)
+
+    def got(sem, ref):
+        remote(ref, ref, cs.at[0], sem, sibling).wait_recv()
+
+    v_chunk, a_chunk = vbuf.at[0, pl.ds(0, TILE)], abuf.at[0, pl.ds(0, ACH)]
 
     def pair_copy(i, y):
         t = a_at(z, y, i)
@@ -203,7 +197,7 @@
         near = where([(dx == 0, 0), (dx == 1, 9 - tile), (dx == 3, tile + 1), (tile < 5, tile + 10)], 18 - tile)
         far = where(
             [(dx == 0, pos + YLAG + 1), (dx == 1, jnp.where(tile < 5, 18 - tile, fall)),
-             (dx == 3, jnp.where(low, rise, tile + 11))],
+             (dx == 3, jnp.where(low, rise, tile + 11)), (tile < 3, tile + 20)],
             99)
         return jnp.where(jh == h, near, far)
 
@@ -226,28 +220,6 @@
     def group(q, groups):
         return where([(q == last, n) for last, n in groups.items()], 0)
 
-    def zstep(r, _):
-        z_arrival(r, 0).wait_recv()
-        z_arrival(r, 1).wait_recv()
-
-        @pl.when(r < 3)
-        def _():
-            pair_copy(r, 1 - yl).wait_recv()
-
-        @pl.when(r + ZAHEAD < QZ)
-        def _():
-            z_copy(r + ZAHEAD, 0).start()
-
-        @pl.when((r + ZAHEAD < QZ) & (r != 16))
-        def _():
-            @pl.when(r == 17)
-            def _():
-                z_copy(r + ZAHEAD - 1, 1).start()
-
-            z_copy(r + ZAHEAD, 1).start()
-
-        return 0
-
     def send(copy, lo, hi):
         def one(q, _):
             copy(q).start()
@@ -255,20 +227,39 @@
 
         lax.fori_loop(lo, hi, one, 0)
 
+    def z_sent(r, here):
+        out = jnp.minimum(r + 1 + ZAHEAD, QZ)
+        for q, step in enumerate(here):
+            if step > q - ZAHEAD:
+                out = jnp.minimum(out, jnp.where(r >= step, QZ, q))
+        return out
+
+    def zstep(r, _):
+        got(zr.at[0, lax.rem(r, ZSEM)], a_chunk)
+        got(zr.at[1, lax.rem(r, ZSEM)], a_chunk)
+
+        @pl.when(r < 3)
+        def _():
+            got(pr.at[r], a_chunk)
+
+        send(lambda q: z_copy(q, 0), z_sent(r - 1, ZP_HERE), z_sent(r, ZP_HERE))
+        send(lambda q: z_copy(q, 1), z_sent(r - 1, ZM_HERE), z_sent(r, ZM_HERE))
+        return 0
+
     def slot(t, _):
         p = t - YLAG
 
         @pl.when(t < QX)
         def _():
-            xp_copy(t, 3).wait_recv()
-            sib_copy(0, t, c).start()
-            xm_copy(t, 1).wait_recv()
-            sib_copy(1, t, c).start()
+            got(xr.at[0, lax.rem(t, XSEM)], v_chunk)
+            sib_copy(0, t).start()
+            got(xr.at[1, lax.rem(t, XSEM)], v_chunk)
+            sib_copy(1, t).start()
 
         @pl.when((p >= 0) & (p < QY))
         def _():
-            y_copy(p, 1).wait_recv()
-            sib_copy(2, p, c).start()
+            got(yr.at[p], v_chunk)
+            sib_copy(2, p).start()
 
         send(xp_copy, x_sent(t - 1, XP_HERE), x_sent(t, XP_HERE))
         send(xm_copy, x_sent(t - 1, XM_HERE), x_sent(t, XM_HERE))
@@ -281,12 +272,12 @@
 
         @pl.when((t >= 1) & (t <= QX))
         def _():
-            sib_copy(0, t - 1, 1 - c).wait_recv()
-            sib_copy(1, t - 1, 1 - c).wait_recv()
+            got(cr.at[0, lax.rem(t - 1, CSEM)], v_chunk)
+            got(cr.at[1, lax.rem(t - 1, CSEM)], v_chunk)
 
         @pl.when((p >= 1) & (p <= QY))
         def _():
-            sib_copy(2, p - 1, 1 - c).wait_recv()
+            got(cr.at[2, lax.rem(p - 1, CSEM)], v_chunk)
 
         def fresh(i):
             q = jnp.where(i == 2, p - 1, t - 1)
@@ -341,8 +332,8 @@
 
     lax.fori_loop(0, SLOTS, slot, 0)
 
-    z_arrival(jnp.int32(QZ - 1), 0).wait_recv()
-    z_arrival(jnp.int32(QZ - 1), 1).wait_recv()
+    got(zr.at[0, (QZ - 1) % ZSEM], a_chunk)
+    got(zr.at[1, (QZ - 1) % ZSEM], a_chunk)
 
     def left_all(ref, sem, to):
         remote(ref, ref, sem, orr.at[0], to).wait_send()
@@ -366,25 +357,29 @@
         cols = pl.ds(lo * TILE, (hi - lo) * TILE)
         copies.append(pltpu.make_async_copy(out.at[:, cols], o_ref.at[:, cols], sem.at[g]))
 
-    def run(blocks):
+    def part(g, blocks):
         planes = [2 * j + i for j in blocks for i in range(2)]
+        lo, hi = CUTS[g]
+        rows = pl.ds(lo * TILE, (hi - lo) * TILE)
         a = jnp.concatenate([abuf[k] for k in planes], axis=1)
-        for (lo, hi), copy in zip(CUTS, copies):
-            rows = pl.ds(lo * TILE, (hi - lo) * TILE)
-            b = jnp.concatenate([vbuf[k, rows] for k in planes], axis=1)
-            part = lax.dot_general(a, b, (((1,), (1,)), ((), ())), preferred_element_type=jnp.float32)
-            for tile in range(lo, hi):
-                cols = slice((tile - lo) * TILE, (tile - lo + 1) * TILE)
-                out[:, tile * TILE : (tile + 1) * TILE] = (acc[tile] + part[:, cols]).astype(out.dtype)
-            copy.start()
+        b = jnp.concatenate([vbuf[k, rows] for k in planes], axis=1)
+        summed = lax.dot_general(a, b, (((1,), (1,)), ((), ())), preferred_element_type=jnp.float32)
+        for tile in range(lo, hi):
+            cols = slice((tile - lo) * TILE, (tile - lo + 1) * TILE)
+            out[:, tile * TILE : (tile + 1) * TILE] = (acc[tile] + summed[:, cols]).astype(out.dtype)
+        copies[g].start()
+
+    part(0, [far_a])
 
     @pl.when(far_a == far_v)
     def _():
-        run([far_a])
+        for g in range(1, len(CUTS)):
+            part(g, [far_a])
 
     @pl.when(far_a != far_v)
     def _():
-        run([far_a, far_v])
+        for g in range(1, len(CUTS)):
+            part(g, [far_a, far_v])
 
     for copy in copies:
         copy.wait()

time: 52.1 us -> 52 us (level)
  no operation moved by 1% of the time
where the time goes in v5:
time: 52 us; the launch traced here: 51.9 us
  Pallas kernels  51.9 us (100%)
    pallas_call x1, Pallas kernels, on_device(): pl.pallas_call(kernel, out_shape=[pltpu.VMEM((16, COLS, BLK), jnp.bfloat1...  48.7 us
    pallas_call x1, Pallas kernels, on_device(): pl.pallas_call(finish, out_shape=jax.ShapeDtypeStruct((ROWS, COLS), jnp.b...  3.2 us

profile of v5, /device:TPU:1, one launch (start us, length us, event | category | flops | bytes accessed | tf_op | source)
XLA Modules:
  0.0 51.9 jit_solution(16585473353987541686)
XLA Ops:
  0.0 48.7 %ladder.1 = (bf16[16,2304,128]{2,1,0:T(8,128)(2,1)S(1)}, bf16[16,864,128]{2,1,0:T(8,128)(2,1)S(1)}, f32[9,864,256]{2,1,0:T(8,128)S(1)}) custom-call(bf16[2304,128]{1,0:T(8,128)(2,1)} %v_ref.1, bf16[864,128]{1,0:T(8,128)(2,1)} %r_ref.1), custom_call_target="tpu_custom_call" | custom-call | flops 6115295232 | bytes 1048576 | tf_op jit(solution)/shard_map/ladder/pallas_call | solution.py:391
  48.7 3.2 %finish.1 = bf16[864,2304]{1,0:T(8,128)(2,1)} custom-call(bf16[16,2304,128]{2,1,0:T(8,128)(2,1)S(1)} %get-tuple-element.8.vbuf, bf16[16,864,128]{2,1,0:T(8,128)(2,1)S(1)} %get-tuple-element.9.abuf, f32[9,864,256]{2,1,0:T(8,128)S(1)} %get-tuple-element.10.acc), custom_call_target="tpu_custom_call" | custom-call | flops 2038431744 | bytes 4194304 | tf_op jit(solution)/shard_map/finish/pallas_call | solution.py:418

commit v6 on v5

--- a/solution.py
+++ b/solution.py
@@ -184,7 +184,7 @@
 
     def a_slot(j):
         d = lax.rem(j - z + 8, 8)
-        d = jnp.minimum(d, 8 - d)
+        d = where([(d < 5, d), (d == 5, 4)], 8 - d)
         return where([(d == 0, OWN_SLOT), (d == 1, A_SLOTS[0]), (d == 2, A_SLOTS[1]), (d == 3, A_SLOTS[2])], SLOTS)
 
     def came(j, tile):
@@ -297,7 +297,7 @@
 
         event = where([(t < A_SLOTS[0], OWN_SLOT), (t < A_SLOTS[1], A_SLOTS[0]), (t < A_SLOTS[2], A_SLOTS[1])], A_SLOTS[2])
         dist = where([(t < A_SLOTS[0], 0), (t < A_SLOTS[1], 1), (t < A_SLOTS[2], 2)], 3)
-        busy = where([(dist == 0, t == event), (dist == 1, (t == event) | (t == event + 2)), (dist == 2, (t == event + 2) | (t == event + 3))], (t == event) | (t == event + 1))
+        busy = where([(dist == 0, t == event), (dist == 1, (t == event) | (t == event + 2)), (dist == 2, (t == event + 2) | (t == event + 3))], t == event)
 
         def waited(i):
             j = lax.rem(z + jnp.where((t == event) | ((dist == 2) & (t == event + 2)), dist, 8 - dist), 8)
@@ -369,17 +369,19 @@
             out[:, tile * TILE : (tile + 1) * TILE] = (acc[tile] + summed[:, cols]).astype(out.dtype)
         copies[g].start()
 
-    part(0, [far_a])
-
-    @pl.when(far_a == far_v)
+    late_a = lax.rem(z + 5, 8)
+    both = (far_a == far_v) | (late_a == far_v)
+    part(0, [far_a, late_a])
+
+    @pl.when(both)
     def _():
         for g in range(1, len(CUTS)):
-            part(g, [far_a])
-
-    @pl.when(far_a != far_v)
+            part(g, [far_a, late_a])
+
+    @pl.when(jnp.logical_not(both))
     def _():
         for g in range(1, len(CUTS)):
-            part(g, [far_a, far_v])
+            part(g, [far_a, late_a, far_v])
 
     for copy in copies:
         copy.wait()

time: 52 us -> 51.5 us (level)
  Pallas kernels: 51.9 us -> 51.2 us
    pallas_call x1, Pallas kernels: 48.7 us -> 47.1 us  [on_device(): pl.pallas_call(kernel, out_shape=[pltpu.VMEM((16, COLS, BLK), jnp.bfloat1...]
    pallas_call x1, Pallas kernels: 3.2 us -> 4.11 us  [on_device(): pl.pallas_call(finish, out_shape=jax.ShapeDtypeStruct((ROWS, COLS), jnp.b...]
where the time goes in v6:
time: 51.5 us; the launch traced here: 51.2 us
  Pallas kernels  51.2 us (99%)
    pallas_call x1, Pallas kernels, on_device(): pl.pallas_call(kernel, out_shape=[pltpu.VMEM((16, COLS, BLK), jnp.bfloat1...  47.1 us
    pallas_call x1, Pallas kernels, on_device(): pl.pallas_call(finish, out_shape=jax.ShapeDtypeStruct((ROWS, COLS), jnp.b...  4.11 us

profile of v6, /device:TPU:1, one launch (start us, length us, event | category | flops | bytes accessed | tf_op | source)
XLA Modules:
  0.0 51.2 jit_solution(1220310183788913115)
XLA Ops:
  0.0 47.1 %ladder.1 = (bf16[16,2304,128]{2,1,0:T(8,128)(2,1)S(1)}, bf16[16,864,128]{2,1,0:T(8,128)(2,1)S(1)}, f32[9,864,256]{2,1,0:T(8,128)S(1)}) custom-call(bf16[2304,128]{1,0:T(8,128)(2,1)} %v_ref.1, bf16[864,128]{1,0:T(8,128)(2,1)} %r_ref.1), custom_call_target="tpu_custom_call" | custom-call | flops 6115295232 | bytes 1048576 | tf_op jit(solution)/shard_map/ladder/pallas_call | solution.py:393
  47.1 4.1 %finish.1 = bf16[864,2304]{1,0:T(8,128)(2,1)} custom-call(bf16[16,2304,128]{2,1,0:T(8,128)(2,1)S(1)} %get-tuple-element.8.vbuf, bf16[16,864,128]{2,1,0:T(8,128)(2,1)S(1)} %get-tuple-element.9.abuf, f32[9,864,256]{2,1,0:T(8,128)S(1)} %get-tuple-element.10.acc), custom_call_target="tpu_custom_call" | custom-call | flops 2038431744 | bytes 4194304 | tf_op jit(solution)/shard_map/finish/pallas_call | solution.py:420
